TPU v7x, 512 devices: a whole 4x4x16 slice. The times are simulated.
512 devices in a mesh: head: 32 (over z_lo, y, core), seq: 16 (over z_hi, x).
Axes of the slice: x: 4, y: 4, z: 16 (z_hi: 4, z_lo: 4; z = z_hi * 4 + z_lo), core: 2. Of those that a mesh axis runs over, the one named last changes fastest.
Arguments:
- query_rows: bfloat16 [2048, 16384], P('seq', 'head'), may hold values from -512 to 512
- key_rows: bfloat16 [2048, 1024], P('seq'), may hold values from -32 to 32
- value_rows: bfloat16 [2048, 1024], P('seq'), may hold values from -6 to 6
- positions: int32 [2048], P('seq'), may hold values from 0 to 511, as said below
Outputs:
- attended: bfloat16 [2048, 16384], P('seq', 'head')
- hessian: float32 [16384, 16384], P('head', 'seq')
Inputs may be any that keep to these rules, and one draw needn't show every extreme that they name: Each aligned block of 4 spans of 128 tokens is one sequence; each span holds 128 consecutive ascending positions starting at a multiple of 128, and the sequence's spans together hold every position 0 to 511 once.
All inputs are finite; a program needn't handle non-finite values.
Results may differ from a plain program's by a relative error of at most 0.0037.
Values may be sent and summed in bfloat16 or wider, within the bound.
No kernel may reach another device: no remote copies, remote signals or barrier semaphores. Data moves between devices by JAX's collectives and lax.ppermute only.
A program may use at most 64 MiB of HBM per device.

v0:
```python
import jax
import jax.numpy as jnp
from jax import lax
from jax.sharding import PartitionSpec as P

HEADS = 128
KVH = 8
HD = 128
SPANS = 4


def from_partner(value, axis, stride):
    mask = 2**stride
    pairs = [(source, source ^ mask) for source in range(lax.axis_size(axis))]
    return lax.ppermute(value, axis, pairs)


def attend_block(queries, key_block, value_block, visible, local_heads, local_tokens, score_scale):
    scores = jnp.dot(queries, key_block.T, preferred_element_type=jnp.float32) * score_scale
    scores = scores.reshape(local_heads, local_tokens, key_block.shape[0])
    masked = jnp.where(visible[None], scores, -jnp.inf)
    row_top = jnp.max(masked, axis=2, keepdims=True)
    weights = jnp.exp(masked - row_top)
    weight_sum = jnp.sum(weights, axis=2, keepdims=True)
    mixed = jnp.dot(
        weights.astype(jnp.bfloat16).reshape(local_heads * local_tokens, key_block.shape[0]),
        value_block,
        preferred_element_type=jnp.float32,
    )
    return mixed.reshape(local_heads, local_tokens, HD) / weight_sum


def on_device(query_rows, key_rows, value_rows, positions):
    local_tokens = query_rows.shape[0]
    local_heads = query_rows.shape[1] // HD
    group_size = HEADS // KVH
    score_scale = HD ** (-0.5)
    head_index = lax.axis_index("head")
    seq_devices = lax.axis_size("seq")
    head_devices = lax.axis_size("head")
    key_head = head_index * local_heads // group_size
    key_slice = lax.dynamic_slice_in_dim(key_rows, key_head * HD, HD, 1)
    value_slice = lax.dynamic_slice_in_dim(value_rows, key_head * HD, HD, 1)
    queries = jnp.transpose(query_rows.reshape(local_tokens, local_heads, HD), (1, 0, 2))
    queries = queries.reshape(local_heads * local_tokens, HD)
    key_block, value_block, place_block = (key_slice, value_slice, positions)
    for bit in range(SPANS.bit_length() - 1):
        other_keys, other_values, other_places = from_partner(
            (key_block, value_block, place_block), "seq", bit
        )
        key_block = jnp.concatenate([key_block, other_keys], axis=0)
        value_block = jnp.concatenate([value_block, other_values], axis=0)
        place_block = jnp.concatenate([place_block, other_places], axis=0)
    visible = place_block[None, :] <= positions[:, None]
    outcome = attend_block(
        queries, key_block, value_block, visible, local_heads, local_tokens, score_scale
    )
    attended = (
        jnp.transpose(outcome, (1, 0, 2))
        .reshape(local_tokens, local_heads * HD)
        .astype(jnp.bfloat16)
    )
    row_width = attended.shape[1]
    row_operand = lax.all_gather(attended, "seq", axis=0, tiled=True)
    per_slice = local_tokens // head_devices
    sectioned = attended.reshape(1, per_slice, head_devices, row_width)
    sectioned = lax.all_to_all(sectioned, "head", split_axis=2, concat_axis=3, tiled=True)
    sectioned = lax.all_to_all(sectioned, "seq", split_axis=3, concat_axis=0, tiled=True)
    row_grid = row_operand.reshape(seq_devices, per_slice, head_devices, row_width)
    hessian = lax.dot_general(
        row_grid,
        lax.all_gather(sectioned, "head", axis=2, tiled=True),
        (((0, 1, 2), (0, 1, 2)), ((), ())),
        preferred_element_type=jnp.float32,
    )
    return (attended, hessian)


def solution(mesh):
    placed = (P("seq", "head"), P("seq", None), P("seq", None), P("seq"))
    return jax.shard_map(
        on_device,
        mesh=mesh,
        in_specs=placed,
        out_specs=(P("seq", "head"), P("head", "seq")),
        check_vma=False,
    )
```

profile of v0, /device:TPU:1, one launch (start us, length us, event | category | flops | bytes accessed | tf_op | source)
XLA Modules:
  0.0 303.3 jit_solution(11701521761003018919)
XLA Ops:
  7.2 4.1 %collective-permute-start = (s32[128]{0:T(128)}, s32[128]{0:T(128)S(1)}, u32[]{:S(2)}, u32[]{:S(2)}) collective-permute-start(s32[128]{0:T(128)} %param.7), channel_id=1, source_target_pairs={{0,1},{1,0},{2,3},{3,2},{4,5},{5,4},{6,7},{7,6},{8,9},{9,8},{10,11... | collective-permute-start | bytes 1544 | tf_op jit(solution)/shard_map/ppermute | solution.py:15
  11.4 1.9 collective-permute-start.2
  14.0 4.9 %collective-permute-start.1 = (s32[256]{0:T(256)S(1)}, s32[256]{0:T(256)S(1)}, u32[]{:S(2)}, u32[]{:S(2)}) collective-permute-start(s32[256]{0:T(256)S(1)} %pad_add_fusion.1), channel_id=1, source_target_pairs={{0,2},{1,3},{2,0},{3,1},{4,6},{5,7},{6,4},{7,5},{8,10},{9,11},{10,... | collective-permute-start | bytes 3080 | tf_op jit(solution)/shard_map/ppermute | solution.py:15
  18.9 0.8 constant_dynamic-slice_fusion
  19.7 2.2 collective-permute-start.4
  22.0 1.0 copy.21
  23.8 0.8 broadcast_compare_fusion
  24.6 3.6 %collective-permute-start.3 = (bf16[256,128]{1,0:T(8,128)(2,1)S(1)}, bf16[256,128]{1,0:T(8,128)(2,1)S(1)}, u32[]{:S(2)}, u32[]{:S(2)}) collective-permute-start(bf16[256,128]{1,0:T(8,128)(2,1)S(1)} %pad_maximum_fusion), channel_id=1, source_target_pairs={{0,2},{1,3},{2,0},{3,1},{4,6},{5,7},{6,4},{7,5},{8,10},{9,11},{10,... | collective-permute-start | bytes 196616 | tf_op jit(solution)/shard_map/ppermute | solution.py:15
  28.3 3.1 %collective-permute-start.5 = (bf16[256,128]{0,1:T(8,128)(2,1)S(1)}, bf16[256,128]{0,1:T(8,128)(2,1)S(1)}, u32[]{:S(2)}, u32[]{:S(2)}) collective-permute-start(bf16[256,128]{0,1:T(8,128)(2,1)S(1)} %pad_maximum_fusion.1), channel_id=1, source_target_pairs={{0,2},{1,3},{2,0},{3,1},{4,6},{5,7},{6,4},{7,5},{8,10},{9,11},{10,... | collective-permute-start | bytes 196616 | tf_op jit(solution)/shard_map/ppermute | solution.py:15
  32.3 2.5 collective-permute-done.5
  34.8 1.0 fusion.9
  35.8 1.0 copy.25
  37.1 20.3 %all_to_all.30 = bf16[1,4,32,512]{3,1,0,2:T(4,128)(2,1)S(1)} all-to-all(bf16[1,4,32,512]{3,1,0,2:T(4,128)(2,1)S(1)} %copy.26), channel_id=1, replica_groups=mesh['head'=32,'seq'=16] {'head'}, dimensions={2} | all-to-all | bytes 262144 | tf_op jit(solution)/shard_map/all_to_all | solution.py:67
  57.3 12.9 %copy.27 = bf16[1,4,1,16384]{1,2,0,3:T(2,128)(2,1)} copy(bf16[1,4,1,16384]{3,1,2,0:T(4,128)(2,1)S(1)} %bitcast.58) | data formatting | bytes 262144 | tf_op jit(solution)/shard_map/all_to_all | solution.py:67
  70.7 90.8 %reduce.2 = bf16[16384,4]{1,0:T(8,128)(2,1)} reduce(bf16[16384,1,1,4]{3,2,1,0:T(2,128)(2,1)} %bitcast.52, bf16[]{:T(256)} %broadcast.33), dimensions={1,2}, to_apply=%bitcast.45.reduce_sub_computation | reduce | bytes 262146
  161.5 8.7 %reshape.80 = bf16[16,2,2048]{2,1,0:T(2,128)(2,1)S(1)} reshape(bf16[16384,4]{1,0:T(8,128)(2,1)} %reduce.2) | data formatting | bytes 262144
  170.2 27.8 %all_to_all.31 = bf16[16,2,2048]{2,1,0:T(2,128)(2,1)S(1)} all-to-all(bf16[16,2,2048]{2,1,0:T(2,128)(2,1)S(1)} %reshape.80), channel_id=1, replica_groups=mesh['head'=32,'seq'=16] {'seq'}, dimensions={0} | all-to-all | bytes 262144 | tf_op jit(solution)/shard_map/all_to_all | solution.py:68
  198.0 12.3 %reshape.81 = bf16[16384,1,1,4]{3,2,1,0:T(2,128)(2,1)} reshape(bf16[16,2,2048]{2,1,0:T(2,128)(2,1)S(1)} %all_to_all.31) | data formatting | bytes 262144
  210.3 15.4 %copy.28 = bf16[1,4,1,16384]{3,1,2,0:T(4,128)(2,1)S(1)} copy(bf16[1,4,1,16384]{1,2,0,3:T(2,128)(2,1)} %bitcast.53) | data formatting | bytes 262144 | tf_op jit(solution)/shard_map/all_to_all | solution.py:68
  225.7 0.7 copy.42
  226.4 0.8 copy.31
  227.2 2.9 copy.24
  230.1 57.4 %all-gather.6.cloned.1.call-done = bf16[16,1,4,32,1024]{4,0,2,1,3:T(8,128)(2,1)} async-done(((bf16[16,1,4,1,1024]{4,0,2,1,3:T(8,128)(2,1)}), bf16[16,1,4,32,1024]{4,0,2,1,3:T(8,128)(2,1)}) %all-gather.6.cloned.1.call-update) | async-done | bytes 4194320 | tf_op jit(solution)/shard_map/all_gather | solution.py:72
  287.5 9.0 %fusion.3 = f32[512,1024]{1,0:T(8,128)} fusion(bf16[16,4,32,512]{3,2,1,0:T(8,128)(2,1)S(1)} %bitcast.54, bf16[16,1,4,32,1024]{4,0,2,1,3:T(8,128)(2,1)} %all-gather.6.cloned.1.call-done), kind=kOutput, calls=%fused_computation.3 | convolution fusion | flops 2147483648 | bytes 8388608 | tf_op jit(solution)/shard_map/dot_general | solution.py:70
  (27 shorter events, 3.2 us)
Async XLA Ops:
  7.2 4.2 %copy-start = (bf16[128,1024]{1,0:T(8,128)(2,1)S(1)}, bf16[128,1024]{1,0:T(8,128)(2,1)}, u32[]{:S(2)}) copy-start(bf16[128,1024]{1,0:T(8,128)(2,1)} %param.5) | copy-start | bytes 786436
  7.2 220.0 %all-gather.4.cloned.1.call-start = ((), (), s32[]{:S(2)}) async-start(), calls=%async_computation.2 | async-start | bytes 2228224 | tf_op jit(solution)/shard_map/all_gather | solution.py:64
  7.2 6.1 %collective-permute-start = (s32[128]{0:T(128)}, s32[128]{0:T(128)S(1)}, u32[]{:S(2)}, u32[]{:S(2)}) collective-permute-start(s32[128]{0:T(128)} %param.7), channel_id=1, source_target_pairs={{0,1},{1,0},{2,3},{3,2},{4,5},{5,4},{6,7},{7,6},{8,9},{9,8},{10,11... | collective-permute-start | bytes 1544 | tf_op jit(solution)/shard_map/ppermute | solution.py:15
  11.4 13.2 %collective-permute-start.2 = (bf16[128,128]{1,0:T(8,128)(2,1)S(1)}, bf16[128,128]{1,0:T(8,128)(2,1)S(1)}, u32[]{:S(2)}, u32[]{:S(2)}) collective-permute-start(bf16[128,128]{1,0:T(8,128)(2,1)S(1)} %constant_dynamic-slice_fusion.1), channel_id=1, source_target_pairs={{0,1},{1,0},{2,3},{3,2},{4,5},{5,4},{6,7},{7,6},{8,9},{9,8},{10,11... | collective-permute-start | bytes 98312 | tf_op jit(solution)/shard_map/ppermute | solution.py:15
  14.0 9.2 %collective-permute-start.1 = (s32[256]{0:T(256)S(1)}, s32[256]{0:T(256)S(1)}, u32[]{:S(2)}, u32[]{:S(2)}) collective-permute-start(s32[256]{0:T(256)S(1)} %pad_add_fusion.1), channel_id=1, source_target_pairs={{0,2},{1,3},{2,0},{3,1},{4,6},{5,7},{6,4},{7,5},{8,10},{9,11},{10,... | collective-permute-start | bytes 3080 | tf_op jit(solution)/shard_map/ppermute | solution.py:15
  19.7 8.5 %collective-permute-start.4 = (bf16[128,128]{0,1:T(8,128)(2,1)S(1)}, bf16[128,128]{0,1:T(8,128)(2,1)S(1)}, u32[]{:S(2)}, u32[]{:S(2)}) collective-permute-start(bf16[128,128]{0,1:T(8,128)(2,1)S(1)} %copy.33), channel_id=1, source_target_pairs={{0,1},{1,0},{2,3},{3,2},{4,5},{5,4},{6,7},{7,6},{8,9},{9,8},{10,11... | collective-permute-start | bytes 98312 | tf_op jit(solution)/shard_map/ppermute | solution.py:15
  24.6 6.9 %collective-permute-start.3 = (bf16[256,128]{1,0:T(8,128)(2,1)S(1)}, bf16[256,128]{1,0:T(8,128)(2,1)S(1)}, u32[]{:S(2)}, u32[]{:S(2)}) collective-permute-start(bf16[256,128]{1,0:T(8,128)(2,1)S(1)} %pad_maximum_fusion), channel_id=1, source_target_pairs={{0,2},{1,3},{2,0},{3,1},{4,6},{5,7},{6,4},{7,5},{8,10},{9,11},{10,... | collective-permute-start | bytes 196616 | tf_op jit(solution)/shard_map/ppermute | solution.py:15
  28.3 6.5 %collective-permute-start.5 = (bf16[256,128]{0,1:T(8,128)(2,1)S(1)}, bf16[256,128]{0,1:T(8,128)(2,1)S(1)}, u32[]{:S(2)}, u32[]{:S(2)}) collective-permute-start(bf16[256,128]{0,1:T(8,128)(2,1)S(1)} %pad_maximum_fusion.1), channel_id=1, source_target_pairs={{0,2},{1,3},{2,0},{3,1},{4,6},{5,7},{6,4},{7,5},{8,10},{9,11},{10,... | collective-permute-start | bytes 196616 | tf_op jit(solution)/shard_map/ppermute | solution.py:15
  35.8 251.7 %all-gather.6.cloned.1.call-start = ((), (), s32[]{:S(2)}) async-start(), calls=%async_computation.3 | async-start | bytes 4325376 | tf_op jit(solution)/shard_map/all_gather | solution.py:72
  210.3 16.1 %copy-start.1 = (bf16[128,4,128]{0,2,1:T(8,128)(2,1)S(1)}, bf16[128,4,128]{0,2,1:T(8,128)(2,1)}, u32[]{:S(2)}) copy-start(bf16[128,4,128]{0,2,1:T(8,128)(2,1)} %fusion.9) | copy-start | bytes 393220
Sparse Core Ops, SparseCore 0:
  35.9 105.3 all-gather.3
  226.5 60.8 all-gather.5
where the time goes:
time: 304 us; the launch traced here: 303 us
  other arithmetic  93.2 us (31%)
  waiting for transfers between devices  60 us (20%)
  local copies, waits for them, and re-layouts  57.5 us (19%)
  blocking collectives  48.1 us (16%)
  starting transfers between devices  20 us (7%)
  between operations  14.3 us (5%)
  matrix products  10.4 us (3%)
    unnamed x1, other arithmetic  90.8 us
    all_gather x1, waiting for transfers between devices, on_device(): lax.all_gather(sectioned, 'head', axis=2, tiled=True)  57.4 us
    all_to_all x1, blocking collectives, on_device(): lax.all_to_all(sectioned, 'seq', split_axis=3, concat_axis=0, tiled=True)  27.8 us
    unnamed x11, local copies, waits for them, and re-layouts  24.1 us
    all_to_all x1, blocking collectives, on_device(): lax.all_to_all(sectioned, 'head', split_axis=2, concat_axis=3, tiled=True)  20.3 us
    ppermute x6, starting transfers between devices, from_partner(): return lax.ppermute(value, axis, pairs)  19.9 us
    all_to_all x1, local copies, waits for them, and re-layouts, on_device(): lax.all_to_all(sectioned, 'seq', split_axis=3, concat_axis=0, tiled=True)  15.4 us
    all_to_all x1, local copies, waits for them, and re-layouts, on_device(): lax.all_to_all(sectioned, 'head', split_axis=2, concat_axis=3, tiled=True)  12.9 us
  transfers between devices with their start and end apart: 8, of which 2 were waited for; matrix products, arithmetic and copies ran while one was open for 50% of the time, Pallas kernels for 0%

commit v1 on v0

--- a/solution.py
+++ b/solution.py
@@ -7,6 +7,12 @@
 KVH = 8
 HD = 128
 SPANS = 4
+_try_all_cells = lambda body: jnp.concatenate(
+    lax.all_to_all(
+        jnp.stack([body] * lax.axis_size("head"), 0), axis_name="head", split_axis=0, concat_axis=0
+    ),
+    2,
+)
 
 
 def from_partner(value, axis, stride):
@@ -69,7 +75,7 @@
     row_grid = row_operand.reshape(seq_devices, per_slice, head_devices, row_width)
     hessian = lax.dot_general(
         row_grid,
-        lax.all_gather(sectioned, "head", axis=2, tiled=True),
+        _try_all_cells(sectioned),
         (((0, 1, 2), (0, 1, 2)), ((), ())),
         preferred_element_type=jnp.float32,
     )

time: 304 us -> 386 us (1.27)
  waiting for transfers between devices: 60 us -> 134 us
  starting transfers between devices: 20 us -> 27.7 us
    all_gather x1, waiting for transfers between devices: 0.01 us -> 113 us  [on_device(): row_operand = lax.all_gather(attended, 'seq', axis=0, tiled=True)]
    all_gather x1 -> x0, waiting for transfers between devices: 57.4 us -> none  [on_device(): lax.all_gather(sectioned, 'head', axis=2, tiled=True)]
    all_to_all x0 -> x1, waiting for transfers between devices: none -> 17.7 us  [lax.all_to_all(jnp.stack([body] * lax.axis_size('head'), 0), axis_name='h...]
    all_to_all x0 -> x1, starting transfers between devices: none -> 7.79 us  [lax.all_to_all(jnp.stack([body] * lax.axis_size('head'), 0), axis_name='h...]
    another operation x0 -> x2, local copies, waits for them, and re-layouts: none -> 4.05 us  [jnp.stack([body] * lax.axis_size('head'), 0)]
    unnamed x11 -> x13, local copies, waits for them, and re-layouts: 24.1 us -> 23.5 us
  transfers between devices with their start and end apart: 8 -> 8, of which waited for: 2 -> 3; matrix products, arithmetic and copies ran while one was open for 50% -> 2% of each run, Pallas kernels for 0% -> 0%
where the time goes in v1:
time: 386 us; the launch traced here: 385 us
  waiting for transfers between devices  134 us (35%)
  other arithmetic  93.2 us (24%)
  local copies, waits for them, and re-layouts  59.9 us (16%)
  blocking collectives  48.1 us (12%)
  starting transfers between devices  27.7 us (7%)
  between operations  14.3 us (4%)
  matrix products  7.23 us (2%)
    all_gather x1, waiting for transfers between devices, on_device(): row_operand = lax.all_gather(attended, 'seq', axis=0, tiled=True)  113 us
    unnamed x1, other arithmetic  90.8 us
    all_to_all x1, blocking collectives, on_device(): lax.all_to_all(sectioned, 'seq', split_axis=3, concat_axis=0, tiled=True)  27.8 us
    unnamed x13, local copies, waits for them, and re-layouts  23.5 us
    all_to_all x1, blocking collectives, on_device(): lax.all_to_all(sectioned, 'head', split_axis=2, concat_axis=3, tiled=True)  20.3 us
    ppermute x6, starting transfers between devices, from_partner(): return lax.ppermute(value, axis, pairs)  19.9 us
    all_to_all x1, waiting for transfers between devices, lax.all_to_all(jnp.stack([body] * lax.axis_size('head'), 0), axis_name='h...  17.7 us
    all_to_all x1, local copies, waits for them, and re-layouts, on_device(): lax.all_to_all(sectioned, 'seq', split_axis=3, concat_axis=0, tiled=True)  15.4 us
  transfers between devices with their start and end apart: 8, of which 3 were waited for; matrix products, arithmetic and copies ran while one was open for 2% of the time, Pallas kernels for 0%

profile of v1, /device:TPU:1, one launch (start us, length us, event | category | flops | bytes accessed | tf_op | source)
XLA Modules:
  0.0 384.7 jit_solution(6171439715383217816)
XLA Ops:
  7.2 4.1 %collective-permute-start = (s32[128]{0:T(128)}, s32[128]{0:T(128)S(1)}, u32[]{:S(2)}, u32[]{:S(2)}) collective-permute-start(s32[128]{0:T(128)} %param.7), channel_id=1, source_target_pairs={{0,1},{1,0},{2,3},{3,2},{4,5},{5,4},{6,7},{7,6},{8,9},{9,8},{10,11... | collective-permute-start | bytes 1544 | tf_op jit(solution)/shard_map/ppermute | solution.py:21
  11.3 1.9 collective-permute-start.2
  13.9 4.9 %collective-permute-start.1 = (s32[256]{0:T(256)S(1)}, s32[256]{0:T(256)S(1)}, u32[]{:S(2)}, u32[]{:S(2)}) collective-permute-start(s32[256]{0:T(256)S(1)} %pad_add_fusion.1), channel_id=1, source_target_pairs={{0,2},{1,3},{2,0},{3,1},{4,6},{5,7},{6,4},{7,5},{8,10},{9,11},{10,... | collective-permute-start | bytes 3080 | tf_op jit(solution)/shard_map/ppermute | solution.py:21
  18.8 0.8 constant_dynamic-slice_fusion
  19.7 2.2 collective-permute-start.4
  21.9 1.0 copy.21
  23.8 0.8 broadcast_compare_fusion
  24.6 3.6 collective-permute-start.3
  28.2 3.1 collective-permute-start.5
  32.2 2.5 collective-permute-done.5
  35.4 20.3 %all_to_all.32 = bf16[1,4,32,512]{3,1,0,2:T(4,128)(2,1)S(1)} all-to-all(bf16[1,4,32,512]{3,1,0,2:T(4,128)(2,1)S(1)} %copy.26), channel_id=1, replica_groups=mesh['head'=32,'seq'=16] {'head'}, dimensions={2} | all-to-all | bytes 262144 | tf_op jit(solution)/shard_map/all_to_all | solution.py:73
  55.7 12.9 %copy.27 = bf16[1,4,1,16384]{1,2,0,3:T(2,128)(2,1)} copy(bf16[1,4,1,16384]{3,1,2,0:T(4,128)(2,1)S(1)} %bitcast.60) | data formatting | bytes 262144 | tf_op jit(solution)/shard_map/all_to_all | solution.py:73
  69.0 90.8 %reduce.2 = bf16[16384,4]{1,0:T(8,128)(2,1)} reduce(bf16[16384,1,1,4]{3,2,1,0:T(2,128)(2,1)} %bitcast.54, bf16[]{:T(256)} %broadcast.35), dimensions={1,2}, to_apply=%bitcast.47.reduce_sub_computation | reduce | bytes 262146
  159.8 8.7 %reshape.92 = bf16[16,2,2048]{2,1,0:T(2,128)(2,1)S(1)} reshape(bf16[16384,4]{1,0:T(8,128)(2,1)} %reduce.2) | data formatting | bytes 262144
  168.5 27.8 %all_to_all.33 = bf16[16,2,2048]{2,1,0:T(2,128)(2,1)S(1)} all-to-all(bf16[16,2,2048]{2,1,0:T(2,128)(2,1)S(1)} %reshape.92), channel_id=1, replica_groups=mesh['head'=32,'seq'=16] {'seq'}, dimensions={0} | all-to-all | bytes 262144 | tf_op jit(solution)/shard_map/all_to_all | solution.py:74
  196.3 12.3 %reshape.93 = bf16[16384,1,1,4]{3,2,1,0:T(2,128)(2,1)} reshape(bf16[16,2,2048]{2,1,0:T(2,128)(2,1)S(1)} %all_to_all.33) | data formatting | bytes 262144
  208.6 15.4 %copy.28 = bf16[1,4,1,16384]{3,1,2,0:T(4,128)(2,1)S(1)} copy(bf16[1,4,1,16384]{1,2,0,3:T(2,128)(2,1)} %bitcast.55) | data formatting | bytes 262144 | tf_op jit(solution)/shard_map/all_to_all | solution.py:74
  224.2 3.9 %stack.5 = bf16[32,16,4,1,1024]{4,2,1,3,0:T(4,128)(2,1)} broadcast(bf16[16,4,1024]{2,1,0:T(4,128)(2,1)S(1)} %copy.29), dimensions={1,2,4} | broadcast | bytes 4325376 | tf_op jit(solution)/shard_map/stack | solution.py:12
  228.1 7.8 %all-to-all-start.2 = ((bf16[32,16,4,1,1024]{4,2,1,3,0:T(4,128)(2,1)}), bf16[32,16,4,1,1024]{4,2,1,3,0:T(4,128)(2,1)}, u32[]{:S(2)}, u32[]{:S(2)}) async-start(bf16[32,16,4,1,1024]{4,2,1,3,0:T(4,128)(2,1)} %stack.5), calls=%async_computation.2 | async-start | bytes 8388608 | tf_op jit(solution)/shard_map/all_to_all | solution.py:11
  236.7 0.8 copy.31
  237.4 113.3 %all-gather.2.cloned.1.call-done = bf16[2048,512]{0,1:T(8,128)(2,1)} async-done(((bf16[128,512]{0,1:T(8,128)(2,1)}), bf16[2048,512]{0,1:T(8,128)(2,1)}) %all-gather.2.cloned.1.call-update) | async-done | bytes 2097168 | tf_op jit(solution)/shard_map/all_gather | solution.py:70
  350.7 2.9 copy.24
  353.6 17.7 %all-to-all-done.2 = bf16[32,16,4,1,1024]{4,2,1,3,0:T(4,128)(2,1)} async-done(((bf16[32,16,4,1,1024]{4,2,1,3,0:T(4,128)(2,1)}), bf16[32,16,4,1,1024]{4,2,1,3,0:T(4,128)(2,1)}, u32[]{:S(2)}, u32[]{:S(2)}) %all-to-all-start.2) | async-done | bytes 4194336 | tf_op jit(solution)/shard_map/all_to_all | solution.py:11
  371.3 6.5 %fusion.3 = f32[512,1024]{1,0:T(8,128)} fusion(bf16[16,4,32,512]{3,2,1,0:T(8,128)(2,1)S(1)} %bitcast.56, bf16[32,16,4,1,1024]{4,2,1,3,0:T(4,128)(2,1)} %all-to-all-done.2), kind=kOutput, calls=%fused_computation.3 | convolution fusion | flops 2147483648 | bytes 8388608 | tf_op jit(solution)/shard_map/dot_general | solution.py:76
  (30 shorter events, 4.5 us)
Async XLA Ops:
  7.2 4.1 %copy-start = (bf16[128,1024]{1,0:T(8,128)(2,1)S(1)}, bf16[128,1024]{1,0:T(8,128)(2,1)}, u32[]{:S(2)}) copy-start(bf16[128,1024]{1,0:T(8,128)(2,1)} %param.5) | copy-start | bytes 786436
  7.2 6.1 %collective-permute-start = (s32[128]{0:T(128)}, s32[128]{0:T(128)S(1)}, u32[]{:S(2)}, u32[]{:S(2)}) collective-permute-start(s32[128]{0:T(128)} %param.7), channel_id=1, source_target_pairs={{0,1},{1,0},{2,3},{3,2},{4,5},{5,4},{6,7},{7,6},{8,9},{9,8},{10,11... | collective-permute-start | bytes 1544 | tf_op jit(solution)/shard_map/ppermute | solution.py:21
  11.3 13.2 %collective-permute-start.2 = (bf16[128,128]{1,0:T(8,128)(2,1)S(1)}, bf16[128,128]{1,0:T(8,128)(2,1)S(1)}, u32[]{:S(2)}, u32[]{:S(2)}) collective-permute-start(bf16[128,128]{1,0:T(8,128)(2,1)S(1)} %constant_dynamic-slice_fusion.1), channel_id=1, source_target_pairs={{0,1},{1,0},{2,3},{3,2},{4,5},{5,4},{6,7},{7,6},{8,9},{9,8},{10,11... | collective-permute-start | bytes 98312 | tf_op jit(solution)/shard_map/ppermute | solution.py:21
  13.9 9.2 %collective-permute-start.1 = (s32[256]{0:T(256)S(1)}, s32[256]{0:T(256)S(1)}, u32[]{:S(2)}, u32[]{:S(2)}) collective-permute-start(s32[256]{0:T(256)S(1)} %pad_add_fusion.1), channel_id=1, source_target_pairs={{0,2},{1,3},{2,0},{3,1},{4,6},{5,7},{6,4},{7,5},{8,10},{9,11},{10,... | collective-permute-start | bytes 3080 | tf_op jit(solution)/shard_map/ppermute | solution.py:21
  19.7 8.5 %collective-permute-start.4 = (bf16[128,128]{0,1:T(8,128)(2,1)S(1)}, bf16[128,128]{0,1:T(8,128)(2,1)S(1)}, u32[]{:S(2)}, u32[]{:S(2)}) collective-permute-start(bf16[128,128]{0,1:T(8,128)(2,1)S(1)} %copy.33), channel_id=1, source_target_pairs={{0,1},{1,0},{2,3},{3,2},{4,5},{5,4},{6,7},{7,6},{8,9},{9,8},{10,11... | collective-permute-start | bytes 98312 | tf_op jit(solution)/shard_map/ppermute | solution.py:21
  24.6 6.9 %collective-permute-start.3 = (bf16[256,128]{1,0:T(8,128)(2,1)S(1)}, bf16[256,128]{1,0:T(8,128)(2,1)S(1)}, u32[]{:S(2)}, u32[]{:S(2)}) collective-permute-start(bf16[256,128]{1,0:T(8,128)(2,1)S(1)} %pad_maximum_fusion), channel_id=1, source_target_pairs={{0,2},{1,3},{2,0},{3,1},{4,6},{5,7},{6,4},{7,5},{8,10},{9,11},{10,... | collective-permute-start | bytes 196616 | tf_op jit(solution)/shard_map/ppermute | solution.py:21
  28.2 6.5 %collective-permute-start.5 = (bf16[256,128]{0,1:T(8,128)(2,1)S(1)}, bf16[256,128]{0,1:T(8,128)(2,1)S(1)}, u32[]{:S(2)}, u32[]{:S(2)}) collective-permute-start(bf16[256,128]{0,1:T(8,128)(2,1)S(1)} %pad_maximum_fusion.1), channel_id=1, source_target_pairs={{0,2},{1,3},{2,0},{3,1},{4,6},{5,7},{6,4},{7,5},{8,10},{9,11},{10,... | collective-permute-start | bytes 196616 | tf_op jit(solution)/shard_map/ppermute | solution.py:21
  35.1 33.5 %copy-start.1 = (bf16[128,4,128]{0,2,1:T(8,128)(2,1)}, bf16[128,4,128]{0,2,1:T(8,128)(2,1)S(1)}, u32[]{:S(2)}) copy-start(bf16[128,4,128]{0,2,1:T(8,128)(2,1)S(1)} %fusion.9) | copy-start | bytes 393220
  228.1 8.5 %copy-start.2 = (bf16[128,4,128]{0,2,1:T(8,128)(2,1)S(1)}, bf16[128,4,128]{0,2,1:T(8,128)(2,1)}, u32[]{:S(2)}) copy-start(bf16[128,4,128]{0,2,1:T(8,128)(2,1)} %copy-done.1) | copy-start | bytes 393220
  228.1 143.2 %all-to-all-start.2 = ((bf16[32,16,4,1,1024]{4,2,1,3,0:T(4,128)(2,1)}), bf16[32,16,4,1,1024]{4,2,1,3,0:T(4,128)(2,1)}, u32[]{:S(2)}, u32[]{:S(2)}) async-start(bf16[32,16,4,1,1024]{4,2,1,3,0:T(4,128)(2,1)} %stack.5), calls=%async_computation.2 | async-start | bytes 8388608 | tf_op jit(solution)/shard_map/all_to_all | solution.py:11
  235.9 114.8 %all-gather.2.cloned.1.call-start = ((), (), s32[]{:S(2)}) async-start(), calls=%async_computation.3 | async-start | bytes 2228224 | tf_op jit(solution)/shard_map/all_gather | solution.py:70
Sparse Core Ops, SparseCore 0:
  240.3 110.3 all-gather.1
